TPU v7x, 32 devices: a whole 2x2x4 slice. The times are simulated.
32 devices in a mesh: dp: 2 (over x), seq: 16 (over z, y, core).
Axes of the slice: x: 2, y: 2, z: 4, core: 2. Of those that a mesh axis runs over, the one named last changes fastest.
Arguments:
- tokens: bfloat16 [2, 2048, 1280], P('dp', 'seq'), may hold values from -6 to 6
- place: int32 [16, 128], P('seq'), may hold values from 0 to 127, each once within a row
- kernel: float32 [27, 1280], replicated, may hold values from -1.25 to 1.25
- proj_weight: bfloat16 [1280, 3840], P('seq'), may hold values from -0.15625 to 0.15625
- d_projected: bfloat16 [2, 2048, 3840], P('dp', 'seq'), may hold values from -6 to 6
Outputs:
- projected: bfloat16 [2, 2048, 3840], P('dp', 'seq')
- d_tokens: bfloat16 [2, 2048, 1280], P('dp', 'seq')
- d_kernel: float32 [27, 1280], replicated
Inputs may be any that keep to these rules, and one draw needn't show every extreme that they name: Each row of place holds every number 0 to 127 once.
All inputs are finite; a program needn't handle non-finite values.
Results may differ from a plain program's by a relative error of at most 0.005.
Values may be sent and summed in bfloat16 or wider, within the bound.
A program may use at most 128 MiB of HBM per device.

v0:
```python
import jax
import jax.numpy as jnp
from jax import lax
from jax.sharding import PartitionSpec as P

INLINE = 8
CROSS = 8


def with_halo(value, sides, width):
    for axis, dim in sides:
        size, length = (lax.axis_size(axis), value.shape[dim])
        up = [(i, (i + 1) % size) for i in range(size - 1)]
        down = [(j, i) for i, j in up]
        last = lax.slice_in_dim(value, length - width, length, axis=dim)
        first = lax.slice_in_dim(value, 0, width, axis=dim)
        before = lax.ppermute(last, axis, up)
        after = lax.ppermute(first, axis, down)
        value = jnp.concatenate([before, value, after], axis=dim)
    return value


def brick_cells(landed, inverse):
    tokens_dev = inverse.shape[0]
    width = landed.shape[-1]
    slots = landed.reshape(tokens_dev, width)
    cells = jnp.take(slots, inverse, axis=0)
    return cells.reshape(tokens_dev // (INLINE * CROSS), INLINE, CROSS, width)


def scan_pieces(cells, order, count):
    width = cells.shape[-1]
    tokens_dev = order.shape[0]
    slots = jnp.take(cells.reshape(tokens_dev, width), order, axis=0)
    return slots.reshape(count, tokens_dev // count, width)


def to_bricks(rows, inverse, count):
    tokens_dev, width = rows.shape
    landed = lax.all_to_all(
        rows.reshape(count, tokens_dev // count, width),
        "seq",
        split_axis=0,
        concat_axis=0,
        tiled=True,
    )
    return brick_cells(landed, inverse)


def to_scan(cells, order, count):
    landed = lax.all_to_all(
        scan_pieces(cells, order, count), "seq", split_axis=0, concat_axis=0, tiled=True
    )
    return landed.reshape(order.shape[0], cells.shape[-1])


def with_faces(block):
    deeper = with_halo(block, (("seq", 0),), 1)
    return jnp.pad(deeper, ((0, 0), (1, 1), (1, 1), (0, 0)))


def window(field, depth_dev, start_z, start_i, start_c):
    return field[
        start_z : start_z + depth_dev, start_i : start_i + INLINE, start_c : start_c + CROSS
    ].astype(jnp.float32)


def forward_conv(grid_x, pad_x, kernel, depth_dev):
    conv = jnp.zeros(grid_x.shape, jnp.float32)
    for offset in range(27):
        conv = conv + kernel[offset] * window(
            pad_x, depth_dev, offset // 9, offset // 3 % 3, offset % 3
        )
    return (grid_x.astype(jnp.float32) + conv).astype(jnp.bfloat16)


def backward_conv(grid_d, pad_d, pad_x, kernel, depth_dev):
    grid_float = grid_d.astype(jnp.float32)
    back = grid_float
    partial_value = []
    for offset in range(27):
        dz, di, dc = (offset // 9, offset // 3 % 3, offset % 3)
        back = back + kernel[offset] * window(pad_d, depth_dev, 2 - dz, 2 - di, 2 - dc)
        partial_value.append(
            jnp.sum(grid_float * window(pad_x, depth_dev, dz, di, dc), axis=(0, 1, 2))
        )
    return (back.astype(jnp.bfloat16), jnp.stack(partial_value))


def shards(tokens, place, kernel, proj_weight, d_projected):
    count = lax.axis_size("seq")
    order = place[0]
    inverse = jnp.argsort(order)
    rows_x = tokens[0]
    d_rows = d_projected[0]
    depth_dev = rows_x.shape[0] // (INLINE * CROSS)
    d_y = lax.dot_general(
        d_rows,
        lax.all_gather(proj_weight, "seq", axis=0, tiled=True),
        (((1,), (1,)), ((), ())),
        preferred_element_type=jnp.float32,
    )
    d_y = d_y.astype(jnp.bfloat16)
    grid_x = to_bricks(rows_x, inverse, count)
    pad_x = with_faces(grid_x)
    grid_y = forward_conv(grid_x, pad_x, kernel, depth_dev)
    rows_y = to_scan(grid_y, order, count)
    grid_d = to_bricks(d_y, inverse, count)
    pad_d = with_faces(grid_d)
    back, partial_value = backward_conv(grid_d, pad_d, pad_x, kernel, depth_dev)
    d_tokens = to_scan(back, order, count)
    projected = jnp.dot(
        rows_y,
        lax.all_gather(proj_weight, "seq", axis=0, tiled=True),
        preferred_element_type=jnp.float32,
    )
    projected = projected.astype(jnp.bfloat16)
    d_kernel = lax.psum(partial_value, ("dp", "seq"))
    return (projected[None], d_tokens[None], d_kernel)


def solution(mesh):
    placed = (P("dp", "seq", None), P("seq", None), P(), P("seq", None), P("dp", "seq", None))
    return jax.shard_map(
        shards,
        mesh=mesh,
        in_specs=placed,
        out_specs=(P("dp", "seq", None), P("dp", "seq", None), P()),
        check_vma=False,
    )
```

profile of v0, /device:TPU:0, one launch (start us, length us, event | category | flops | bytes accessed | tf_op | source)
XLA Modules:
  0.0 306.6 jit_solution(7513265851473466111)
XLA Ops:
  7.9 7.4 %all-to-all-start = ((bf16[16,8,1280]{2,1,0:T(8,128)(2,1)}), bf16[16,8,1280]{2,1,0:T(8,128)(2,1)S(1)}, u32[]{:S(2)}, u32[]{:S(2)}) async-start(bf16[16,8,1280]{2,1,0:T(8,128)(2,1)} %bitcast.72), calls=%async_computation | async-start | bytes 655360 | tf_op jit(solution)/shard_map/all_to_all | solution.py:40
  15.3 3.2 %sort.17 = (s32[128]{0:T(128)}, s32[128]{0:T(128)S(1)}) sort(s32[128]{0:T(128)} %bitcast.73, s32[128]{0:T(128)S(1)} %iota.4), dimensions={0}, to_apply=%region_0.0 | sort | flops 896 | bytes 2048 | tf_op jit(solution)/shard_map/jit(argsort)/sort | solution.py:93
  18.5 1.9 slice_reduce_fusion.25
  21.1 77.0 %all-gather.2.cloned.1.call-done = bf16[1280,3840]{1,0:T(8,128)(2,1)} async-done(((bf16[80,3840]{1,0:T(8,128)(2,1)}), bf16[1280,3840]{1,0:T(8,128)(2,1)}) %all-gather.2.cloned.1.call-update) | async-done | bytes 9830416 | tf_op jit(solution)/shard_map/all_gather | solution.py:114
  98.1 7.8 %fusion.4 = bf16[16,8,1280]{2,1,0:T(8,128)(2,1)} fusion(bf16[1280,3840]{1,0:T(8,128)(2,1)} %all-gather.2.cloned.1.call-done, bf16[1,128,3840]{2,1,0:T(8,128)(2,1)S(1)} %copy-done), kind=kOutput, calls=%fused_computation.42 | convolution fusion | flops 1258455040 | bytes 11141120 | tf_op jit(solution)/shard_map/dot_general | solution.py:97
  105.9 3.5 %all-to-all-start.2 = ((bf16[16,8,1280]{2,1,0:T(8,128)(2,1)}), bf16[16,8,1280]{2,1,0:T(8,128)(2,1)S(1)}, u32[]{:S(2)}, u32[]{:S(2)}) async-start(bf16[16,8,1280]{2,1,0:T(8,128)(2,1)} %fusion.4), calls=%async_computation.2 | async-start | bytes 655360 | tf_op jit(solution)/shard_map/all_to_all | solution.py:40
  112.3 8.2 %all-to-all-done.2 = bf16[16,8,1280]{2,1,0:T(8,128)(2,1)S(1)} async-done(((bf16[16,8,1280]{2,1,0:T(8,128)(2,1)}), bf16[16,8,1280]{2,1,0:T(8,128)(2,1)S(1)}, u32[]{:S(2)}, u32[]{:S(2)}) %all-to-all-start.2) | async-done | bytes 327712 | tf_op jit(solution)/shard_map/all_to_all | solution.py:40
  121.8 1.8 collective-permute-start
  126.3 3.7 %collective-permute-start.2 = (bf16[1,8,8,1280]{3,2,1,0:T(8,128)(2,1)}, bf16[1,8,8,1280]{3,2,1,0:T(8,128)(2,1)}, u32[]{:S(2)}, u32[]{:S(2)}) collective-permute-start(bf16[1,8,8,1280]{3,2,1,0:T(8,128)(2,1)} %get-tuple-element.68), channel_id=1, source_target_pairs={{0,1},{1,2},{2,3},{3,4},{4,5},{5,6},{6,7},{7,8},{8,9},{9,10},{10,1... | collective-permute-start | bytes 491528 | tf_op jit(solution)/shard_map/ppermute | solution.py:17
  132.0 2.5 fusion.84
  134.5 1.7 gather_fusion.1
  137.7 3.4 %add_convert_fusion = bf16[2,8,8,1280]{3,2,1,0:T(8,128)(2,1)S(1)} fusion(bf16[2,8,8,1280]{3,2,1,0:T(8,128)(2,1)S(1)} %bitcast.67, bf16[4,10,10,1280]{3,2,1,0:T(8,128)(2,1)S(1)} %select_maximum_fusion, bf16[1,8,8,1280]{3,2,1,0:T(8,128)(2,1)} %collective-permute-done.2, bf16[1,8,8,1280]{3,2,1,0:T(8,128)(2,1)} %collective-permute-done.3, ...), kind=kLoop, calls=%fused_computation.155 | loop fusion | flops 13762560 | bytes 8985600 | tf_op jit(solution)/shard_map/convert_element_type | solution.py:87
  141.2 1.7 gather_fusion.3
  142.9 2.1 select_bitcast_fusion
  145.0 7.6 %all-to-all-start.1 = ((bf16[16,8,1280]{2,1,0:T(8,128)(2,1)}), bf16[16,8,1280]{2,1,0:T(8,128)(2,1)S(1)}, u32[]{:S(2)}, u32[]{:S(2)}) async-start(bf16[16,8,1280]{2,1,0:T(8,128)(2,1)} %get-tuple-element.73), calls=%async_computation.1 | async-start | bytes 655360 | tf_op jit(solution)/shard_map/all_to_all | solution.py:51
  152.6 1.7 fusion.79
  154.4 1.8 fusion.83
  156.3 7.4 %all-to-all-done.1 = bf16[16,8,1280]{2,1,0:T(8,128)(2,1)S(1)} async-done(((bf16[16,8,1280]{2,1,0:T(8,128)(2,1)}), bf16[16,8,1280]{2,1,0:T(8,128)(2,1)S(1)}, u32[]{:S(2)}, u32[]{:S(2)}) %all-to-all-start.1) | async-done | bytes 327712 | tf_op jit(solution)/shard_map/all_to_all | solution.py:51
  163.7 3.5 %all-to-all-start.3 = ((bf16[16,8,1280]{2,1,0:T(8,128)(2,1)}), bf16[16,8,1280]{2,1,0:T(8,128)(2,1)S(1)}, u32[]{:S(2)}, u32[]{:S(2)}) async-start(bf16[16,8,1280]{2,1,0:T(8,128)(2,1)} %get-tuple-element.72), calls=%async_computation.3 | async-start | bytes 655360 | tf_op jit(solution)/shard_map/all_to_all | solution.py:51
  167.5 2.7 stack.111
  170.2 6.2 %fusion = bf16[1,128,3840]{2,1,0:T(8,128)(2,1)} fusion(bf16[1280,3840]{1,0:T(8,128)(2,1)} %all-gather.2.cloned.1.call-done, bf16[16,8,1280]{2,1,0:T(8,128)(2,1)S(1)} %all-to-all-done.1), kind=kOutput, calls=%fused_computation.37 | convolution fusion | flops 1258782720 | bytes 11141120 | tf_op jit(solution)/shard_map/dot_general | solution.py:112
  176.4 1.9 all-to-all-done.3
  178.3 119.1 %all-reduce.4.cloned.1.call-done = f32[27,1280]{1,0:T(8,128)} async-done(((f32[27,1280]{1,0:T(8,128)}), f32[27,1280]{1,0:T(8,128)}) %all-reduce.4.cloned.1.call-update) | async-done | bytes 138256 | tf_op jit(solution)/shard_map/psum | solution.py:118
  298.1 1.6 copy.11
  (92 shorter events, 12.5 us)
Async XLA Ops:
  7.2 91.0 %copy-start = (bf16[1,128,3840]{2,1,0:T(8,128)(2,1)S(1)}, bf16[1,128,3840]{2,1,0:T(8,128)(2,1)}, u32[]{:S(2)}) copy-start(bf16[1,128,3840]{2,1,0:T(8,128)(2,1)} %param.11) | copy-start | bytes 2949124
  7.2 91.0 %all-gather.2.cloned.1.call-start = ((), (), s32[]{:S(2)}) async-start(), calls=%async_computation.4 | async-start | bytes 10444800 | tf_op jit(solution)/shard_map/all_gather | solution.py:114
  7.9 98.0 %all-to-all-start = ((bf16[16,8,1280]{2,1,0:T(8,128)(2,1)}), bf16[16,8,1280]{2,1,0:T(8,128)(2,1)S(1)}, u32[]{:S(2)}, u32[]{:S(2)}) async-start(bf16[16,8,1280]{2,1,0:T(8,128)(2,1)} %bitcast.72), calls=%async_computation | async-start | bytes 655360 | tf_op jit(solution)/shard_map/all_to_all | solution.py:40
  21.1 89.0 %copy-start.3 = (f32[27,1280]{1,0:T(8,128)S(1)}, f32[27,1280]{1,0:T(8,128)}, u32[]{:S(2)}) copy-start(f32[27,1280]{1,0:T(8,128)} %param.9) | copy-start | bytes 414724
  21.1 89.8 %copy-start.18 = (s32[1,128]{1,0:T(1,128)S(1)}, s32[1,128]{1,0:T(1,128)}, u32[]{:S(2)}) copy-start(s32[1,128]{1,0:T(1,128)} %param.8) | copy-start | bytes 1540
  105.9 14.6 %all-to-all-start.2 = ((bf16[16,8,1280]{2,1,0:T(8,128)(2,1)}), bf16[16,8,1280]{2,1,0:T(8,128)(2,1)S(1)}, u32[]{:S(2)}, u32[]{:S(2)}) async-start(bf16[16,8,1280]{2,1,0:T(8,128)(2,1)} %fusion.4), calls=%async_computation.2 | async-start | bytes 655360 | tf_op jit(solution)/shard_map/all_to_all | solution.py:40
  121.4 10.5 %copy-start.4 = (f32[1280]{0:T(1024)S(1)}, f32[1280]{0:T(1024)}, u32[]{:S(2)}) copy-start(f32[1280]{0:T(1024)} %get-tuple-element.52) | copy-start | bytes 15364
  121.4 10.5 %copy-start.5 = (f32[1280]{0:T(1024)S(1)}, f32[1280]{0:T(1024)}, u32[]{:S(2)}) copy-start(f32[1280]{0:T(1024)} %get-tuple-element.53) | copy-start | bytes 15364
  121.4 10.5 %copy-start.6 = (f32[1280]{0:T(1024)S(1)}, f32[1280]{0:T(1024)}, u32[]{:S(2)}) copy-start(f32[1280]{0:T(1024)} %get-tuple-element.54) | copy-start | bytes 15364
  121.4 10.5 %copy-start.7 = (f32[1280]{0:T(1024)S(1)}, f32[1280]{0:T(1024)}, u32[]{:S(2)}) copy-start(f32[1280]{0:T(1024)} %get-tuple-element.55) | copy-start | bytes 15364
  121.5 10.5 %copy-start.8 = (f32[1280]{0:T(1024)S(1)}, f32[1280]{0:T(1024)}, u32[]{:S(2)}) copy-start(f32[1280]{0:T(1024)} %get-tuple-element.56) | copy-start | bytes 15364
  121.5 10.5 %copy-start.9 = (f32[1280]{0:T(1024)S(1)}, f32[1280]{0:T(1024)}, u32[]{:S(2)}) copy-start(f32[1280]{0:T(1024)} %get-tuple-element.57) | copy-start | bytes 15364
  121.5 10.5 %copy-start.10 = (f32[1280]{0:T(1024)S(1)}, f32[1280]{0:T(1024)}, u32[]{:S(2)}) copy-start(f32[1280]{0:T(1024)} %get-tuple-element.58) | copy-start | bytes 15364
  121.5 10.5 %copy-start.11 = (f32[1280]{0:T(1024)S(1)}, f32[1280]{0:T(1024)}, u32[]{:S(2)}) copy-start(f32[1280]{0:T(1024)} %get-tuple-element.59) | copy-start | bytes 15364
  121.5 10.5 %copy-start.12 = (f32[1280]{0:T(1024)S(1)}, f32[1280]{0:T(1024)}, u32[]{:S(2)}) copy-start(f32[1280]{0:T(1024)} %get-tuple-element.60) | copy-start | bytes 15364
  121.8 12.7 %copy-start.1 = (bf16[128,1280]{1,0:T(8,128)(2,1)}, bf16[128,1280]{1,0:T(8,128)(2,1)S(1)}, u32[]{:S(2)}) copy-start(bf16[128,1280]{1,0:T(8,128)(2,1)S(1)} %get-tuple-element.67) | copy-start | bytes 983044
  121.8 9.4 %collective-permute-start = (bf16[1,8,8,1280]{3,2,1,0:T(8,128)(2,1)S(1)}, bf16[1,8,8,1280]{3,2,1,0:T(8,128)(2,1)S(1)}, u32[]{:S(2)}, u32[]{:S(2)}) collective-permute-start(bf16[1,8,8,1280]{3,2,1,0:T(8,128)(2,1)S(1)} %get-tuple-element.71), channel_id=1, source_target_pairs={{0,1},{1,2},{2,3},{3,4},{4,5},{5,6},{6,7},{7,8},{8,9},{9,10},{10,1... | collective-permute-start | bytes 491528 | tf_op jit(solution)/shard_map/ppermute | solution.py:17
  123.6 7.6 %collective-permute-start.1 = (bf16[1,8,8,1280]{3,2,1,0:T(8,128)(2,1)S(1)}, bf16[1,8,8,1280]{3,2,1,0:T(8,128)(2,1)S(1)}, u32[]{:S(2)}, u32[]{:S(2)}) collective-permute-start(bf16[1,8,8,1280]{3,2,1,0:T(8,128)(2,1)S(1)} %get-tuple-element.70), channel_id=1, source_target_pairs={{1,0},{2,1},{3,2},{4,3},{5,4},{6,5},{7,6},{8,7},{9,8},{10,9},{11,1... | collective-permute-start | bytes 491528 | tf_op jit(solution)/shard_map/ppermute | solution.py:18
  126.3 10.0 %collective-permute-start.2 = (bf16[1,8,8,1280]{3,2,1,0:T(8,128)(2,1)}, bf16[1,8,8,1280]{3,2,1,0:T(8,128)(2,1)}, u32[]{:S(2)}, u32[]{:S(2)}) collective-permute-start(bf16[1,8,8,1280]{3,2,1,0:T(8,128)(2,1)} %get-tuple-element.68), channel_id=1, source_target_pairs={{0,1},{1,2},{2,3},{3,4},{4,5},{5,6},{6,7},{7,8},{8,9},{9,10},{10,1... | collective-permute-start | bytes 491528 | tf_op jit(solution)/shard_map/ppermute | solution.py:17
  130.0 6.3 %collective-permute-start.3 = (bf16[1,8,8,1280]{3,2,1,0:T(8,128)(2,1)}, bf16[1,8,8,1280]{3,2,1,0:T(8,128)(2,1)}, u32[]{:S(2)}, u32[]{:S(2)}) collective-permute-start(bf16[1,8,8,1280]{3,2,1,0:T(8,128)(2,1)} %get-tuple-element.69), channel_id=1, source_target_pairs={{1,0},{2,1},{3,2},{4,3},{5,4},{6,5},{7,6},{8,7},{9,8},{10,9},{11,1... | collective-permute-start | bytes 491528 | tf_op jit(solution)/shard_map/ppermute | solution.py:18
  145.0 18.7 %all-to-all-start.1 = ((bf16[16,8,1280]{2,1,0:T(8,128)(2,1)}), bf16[16,8,1280]{2,1,0:T(8,128)(2,1)S(1)}, u32[]{:S(2)}, u32[]{:S(2)}) async-start(bf16[16,8,1280]{2,1,0:T(8,128)(2,1)} %get-tuple-element.73), calls=%async_computation.1 | async-start | bytes 655360 | tf_op jit(solution)/shard_map/all_to_all | solution.py:51
  154.4 13.1 %copy-start.17 = (f32[1,1280]{1,0:T(1,128)S(1)}, f32[1,1280]{1,0:T(1,128)}, u32[]{:S(2)}) copy-start(f32[1,1280]{1,0:T(1,128)} %stack.97) | copy-start | bytes 15364
  163.7 14.6 %all-to-all-start.3 = ((bf16[16,8,1280]{2,1,0:T(8,128)(2,1)}), bf16[16,8,1280]{2,1,0:T(8,128)(2,1)S(1)}, u32[]{:S(2)}, u32[]{:S(2)}) async-start(bf16[16,8,1280]{2,1,0:T(8,128)(2,1)} %get-tuple-element.72), calls=%async_computation.3 | async-start | bytes 655360 | tf_op jit(solution)/shard_map/all_to_all | solution.py:51
  167.2 130.2 %all-reduce.4.cloned.1.call-start = ((), (), s32[]{:S(2)}) async-start(), calls=%async_computation.5 | async-start | bytes 327680 | tf_op jit(solution)/shard_map/psum | solution.py:118
  (5 other events, 42.7 us)
Sparse Core Ops, SparseCore 0:
  10.3 87.7 all-gather.1
  174.2 123.1 all-reduce.3
where the time goes:
time: 309 us; the launch traced here: 307 us
  waiting for transfers between devices  214 us (69%)
  starting transfers between devices  30.2 us (10%)
  other arithmetic  18.7 us (6%)
  local copies, waits for them, and re-layouts  14.6 us (5%)
  between operations  14.6 us (5%)
  matrix products  14 us (5%)
    psum x1, waiting for transfers between devices, shards(): d_kernel = lax.psum(partial_value, ('dp', 'seq'))  119 us
    all_gather x1, waiting for transfers between devices, shards(): lax.all_gather(proj_weight, 'seq', axis=0, tiled=True)  77 us
    all_to_all x2, starting transfers between devices, to_scan(): lax.all_to_all(scan_pieces(cells, order, count), 'seq', split_axis=0, con...  11.1 us
    all_to_all x2, starting transfers between devices, to_bricks(): lax.all_to_all(rows.reshape(count, tokens_dev // count, width), 'seq', sp...  10.9 us
    all_to_all x2, waiting for transfers between devices, to_scan(): lax.all_to_all(scan_pieces(cells, order, count), 'seq', split_axis=0, con...  9.31 us
    all_to_all x2, waiting for transfers between devices, to_bricks(): lax.all_to_all(rows.reshape(count, tokens_dev // count, width), 'seq', sp...  8.2 us
    dot_general x1, matrix products, shards(): lax.dot_general(d_rows, lax.all_gather(proj_weight, 'seq', axis=0, tiled=...  7.77 us
    dot_general x1, matrix products, shards(): jnp.dot(rows_y, lax.all_gather(proj_weight, 'seq', axis=0, tiled=True), p...  6.21 us
  transfers between devices with their start and end apart: 10, of which 5 were waited for; matrix products, arithmetic and copies ran while one was open for 11% of the time, Pallas kernels for 0%

commit v1 on v0

--- a/solution.py
+++ b/solution.py
@@ -1,10 +1,16 @@
+import functools
+
 import jax
 import jax.numpy as jnp
 from jax import lax
+from jax.experimental import pallas as pl
+from jax.experimental.pallas import tpu as pltpu
 from jax.sharding import PartitionSpec as P
 
 INLINE = 8
 CROSS = 8
+MESH = pl.DeviceIdType.MESH
+LANES = 128
 
 
 def with_halo(value, sides, width):
@@ -119,10 +125,471 @@
     return (projected[None], d_tokens[None], d_kernel)
 
 
+def fused(
+    count,
+    tok_ref,
+    row_ref,
+    col_ref,
+    ker_ref,
+    w_ref,
+    dp_ref,
+    proj_ref,
+    dtok_ref,
+    dker_ref,
+    w_all,
+    land,
+    send,
+    edge,
+    halo,
+    field_x,
+    field_d,
+    cells,
+    sums,
+    arrived,
+    move_s,
+    move_r,
+    ring_s,
+    ring_r,
+    part_s,
+    part_r,
+    sib_s,
+    sib_r,
+    halo_s,
+    halo_r,
+    sum_s,
+    sum_r,
+):
+    me = lax.axis_index("seq")
+    plane = lax.axis_index("dp")
+    tokens_dev, width = cells.shape
+    rows = w_ref.shape[0]
+    third = w_ref.shape[1] // 3
+    layer = INLINE * CROSS
+    depth = tokens_dev // layer
+    group = tokens_dev // count
+    chips = count // 2
+    line = chips // 2
+    core = me % 2
+    chip = me // 2
+    chip_y = chip % 2
+    chip_z = chip // 2
+    ring = chip_z * (1 - chip_y) + (chips - 1 - chip_z) * chip_y
+    sibling = me + 1 - 2 * core
+    sign = 1 - 2 * core
+    own_third = pl.multiple_of((1 + plane) * third, LANES)
+    other_third = pl.multiple_of((2 - plane) * third, LANES)
+
+    def at_ring(position):
+        spot = (position + 2 * chips) % chips
+        side = spot // line
+        z = spot * (1 - side) + (chips - 1 - spot) * side
+        return (z * 2 + side) * 2 + core
+
+    def block(shard, start):
+        return w_all.at[pl.ds(pl.multiple_of(shard * rows, 16), rows), pl.ds(start, third)]
+
+    def whole(shard):
+        return w_all.at[pl.ds(pl.multiple_of(shard * rows, 16), rows), :]
+
+    def remote(src, dst, s_sem, r_sem, target):
+        return pltpu.make_async_remote_copy(
+            src_ref=src,
+            dst_ref=dst,
+            send_sem=s_sem,
+            recv_sem=r_sem,
+            device_id=target,
+            device_id_type=MESH,
+        )
+
+    edge_zero = jnp.zeros((layer, width), jnp.bfloat16)
+    for which in range(2):
+        for side in range(2):
+            halo[which, side] = edge_zero
+    w_all[pl.ds(pl.multiple_of(me * rows, 16), rows), :] = w_ref[...]
+
+    barrier = pltpu.get_barrier_semaphore()
+    for step in range(1, count):
+        pl.semaphore_signal(
+            barrier, inc=1, device_id={"seq": (me + step) % count}, device_id_type=MESH
+        )
+    pl.semaphore_signal(barrier, inc=1, device_id={"dp": 1 - plane}, device_id_type=MESH)
+    pl.semaphore_wait(barrier, count)
+
+    sent = []
+
+    def exchange(which, source):
+        copies = []
+        for step in range(1, count):
+            target = (me + step) % count
+            copies.append(
+                remote(
+                    source.at[target],
+                    land.at[which, me],
+                    move_s.at[which, step],
+                    move_r.at[which, step],
+                    {"seq": target},
+                )
+            )
+        for copy in copies:
+            copy.start()
+        sent.extend(copies)
+        land[which, pl.ds(me, 1)] = source[pl.ds(me, 1)]
+        return copies
+
+    def landed(which, copies):
+        for copy in copies:
+            copy.wait_recv()
+        value = land[which].astype(jnp.float32)
+        return value.reshape(tokens_dev, width).astype(jnp.bfloat16)
+
+    def outgoing(which, slots):
+        send[which] = slots.reshape(count, group, width).astype(jnp.bfloat16)
+        return exchange(which, send.at[which])
+
+    move_x = exchange(0, tok_ref)
+
+    hops = (line, chips - 1 - line)
+    signs = (sign, -sign)
+
+    def ring_copies(way, hop):
+        shard = at_ring(ring - signs[way] * (hop - 1))
+        target = {"seq": at_ring(ring + signs[way])}
+        pair = []
+        for piece, start in enumerate((0, own_third)):
+            pair.append(
+                remote(
+                    block(shard, start),
+                    block(shard, start),
+                    ring_s.at[way, hop, piece],
+                    ring_r.at[way, hop, piece],
+                    target,
+                )
+            )
+        return pair
+
+    moving = {}
+    for way in range(2):
+        moving[way, 1] = ring_copies(way, 1)
+    for piece in range(2):
+        for way in range(2):
+            moving[way, 1][piece].start()
+    for way in range(2):
+        sent.extend(moving[way, 1])
+    own_copy = remote(
+        whole(me), whole(me), sib_s.at[0, 0, 0], sib_r.at[0, 0, 0], {"seq": sibling}
+    )
+    own_copy.start()
+    sent.append(own_copy)
+    to_sibling = [own_copy]
+    across = {}
+
+    def sibling_copy(way, hop, piece, shard, start):
+        copy = remote(
+            block(shard, start),
+            block(shard, start),
+            sib_s.at[1 + way, hop, piece],
+            sib_r.at[1 + way, hop, piece],
+            {"seq": sibling},
+        )
+        copy.start()
+        sent.append(copy)
+        to_sibling.append(copy)
+
+    def ring_step(hop):
+        ways = [way for way in range(2) if hop <= hops[way]]
+        for way in ways:
+            if hop < hops[way]:
+                moving[way, hop + 1] = ring_copies(way, hop + 1)
+                sent.extend(moving[way, hop + 1])
+        for piece, start in enumerate((0, own_third)):
+            for way in ways:
+                shard = at_ring(ring - signs[way] * hop)
+                moving[way, hop][piece].wait_recv()
+                if hop < hops[way]:
+                    moving[way, hop + 1][piece].start()
+                if piece == 1:
+                    copy = remote(
+                        block(shard, start),
+                        block(shard, start),
+                        part_s.at[way, hop],
+                        part_r.at[way, hop],
+                        {"dp": 1 - plane},
+                    )
+                    copy.start()
+                    sent.append(copy)
+                    across[way, hop] = copy
+                sibling_copy(way, hop, piece, shard, start)
+
+    def across_step(hop):
+        for way in range(2):
+            if hop <= hops[way]:
+                shard = at_ring(ring - signs[way] * hop)
+                across[way, hop].wait_recv()
+                sibling_copy(way, hop, 2, shard, other_third)
+
+    square = (tokens_dev, tokens_dev)
+    first = lax.broadcasted_iota(jnp.int32, square, 0)
+    second = lax.broadcasted_iota(jnp.int32, square, 1)
+
+    def ones_where(mask):
+        return jnp.where(mask, 1.0, 0.0).astype(jnp.bfloat16)
+
+    to_cells = ones_where(jnp.broadcast_to(row_ref[...], square) == first)
+    to_slots = ones_where(jnp.broadcast_to(col_ref[...], square) == second)
+    spot = first % CROSS
+    shifts = (
+        ones_where((second == first - 1) & (spot > 0)),
+        ones_where((second == first + 1) & (spot < CROSS - 1)),
+    )
+
+    def times(left, right):
+        return jnp.dot(left, right, preferred_element_type=jnp.float32)
+
+    def clear(field):
+        pad = jnp.zeros((CROSS, width), jnp.float32)
+        for shift in range(3):
+            for z in range(depth + 2):
+                field[shift, z, 0] = pad
+                field[shift, z, INLINE + 1] = pad
+
+    def fill(field, layers, value):
+        versions = (times(shifts[0], value), value.astype(jnp.float32), times(shifts[1], value))
+        for shift in range(3):
+            for at, z in enumerate(layers):
+                field[shift, z, pl.ds(1, INLINE)] = versions[shift][
+                    at * layer : (at + 1) * layer
+                ].reshape(INLINE, CROSS, width)
+
+    def halo_pair(which):
+        up = remote(
+            edge.at[which, 0],
+            halo.at[which, 1],
+            halo_s.at[which, 0],
+            halo_r.at[which, 0],
+            {"seq": (me + count - 1) % count},
+        )
+        down = remote(
+            edge.at[which, 1],
+            halo.at[which, 0],
+            halo_s.at[which, 1],
+            halo_r.at[which, 1],
+            {"seq": (me + 1) % count},
+        )
+        return (up, down)
+
+    def halo_start(which, value):
+        edge[which, 0] = value[:layer]
+        edge[which, 1] = value[tokens_dev - layer :]
+        up, down = halo_pair(which)
+
+        @pl.when(me > 0)
+        def _():
+            up.start()
+
+        @pl.when(me < count - 1)
+        def _():
+            down.start()
+
+    def halo_finish(which, field):
+        up, down = halo_pair(which)
+
+        @pl.when(me > 0)
+        def _():
+            down.wait_recv()
+            up.wait_send()
+
+        @pl.when(me < count - 1)
+        def _():
+            up.wait_recv()
+            down.wait_send()
+
+        fill(field, (0, depth + 1), halo[which].reshape(2 * layer, width))
+
+    def window(field, z, i, c, lanes):
+        return field[c, pl.ds(z, depth), pl.ds(i, INLINE), :, lanes]
+
+    def lanes_of(j):
+        return pl.ds(pl.multiple_of(j * LANES, LANES), LANES)
+
+    def convolve(field, flip):
+        def body(j, carry):
+            lanes = lanes_of(j)
+            total = window(field, 1, 1, 1, lanes)
+            for offset in range(27):
+                z, i, c = (offset // 9, offset // 3 % 3, offset % 3)
+                if flip:
+                    z, i, c = (2 - z, 2 - i, 2 - c)
+                total = total + ker_ref[pl.ds(offset, 1), lanes] * window(field, z, i, c, lanes)
+            cells[:, lanes] = total.reshape(tokens_dev, LANES).astype(jnp.bfloat16)
+            return carry
+
+        lax.fori_loop(0, width // LANES, body, 0)
+
+    def kernel_sums():
+        def body(j, carry):
+            lanes = lanes_of(j)
+            grad = window(field_d, 1, 1, 1, lanes)
+            for offset in range(27):
+                z, i, c = (offset // 9, offset // 3 % 3, offset % 3)
+                product = grad * window(field_x, z, i, c, lanes)
+                sums[0, pl.ds(offset, 1), lanes] = jnp.sum(
+                    product.reshape(tokens_dev, LANES), axis=0, keepdims=True
+                )
+            return carry
+
+        lax.fori_loop(0, width // LANES, body, 0)
+
+    own_layers = tuple(range(1, depth + 1))
+    clear(field_x)
+    clear(field_d)
+
+    grid_x = times(to_cells, landed(0, move_x)).astype(jnp.bfloat16)
+    halo_start(0, grid_x)
+    fill(field_x, own_layers, grid_x)
+    ring_step(1)
+    halo_finish(0, field_x)
+    convolve(field_x, False)
+    move_y = outgoing(1, times(to_slots, cells[...]))
+    for hop in range(2, line + 1):
+        ring_step(hop)
+        across_step(hop - 1)
+    across_step(line)
+    for copy in to_sibling:
+        copy.wait_recv()
+
+    tile = 2 * LANES
+
+    def back_body(n, carry):
+        at = pl.multiple_of(n * tile, tile)
+        part = lax.dot_general(
+            dp_ref[...],
+            w_all[pl.ds(at, tile), :],
+            (((1,), (1,)), ((), ())),
+            preferred_element_type=jnp.float32,
+        )
+        send[2, :, :, pl.ds(at, tile)] = part.reshape(count, group, tile).astype(jnp.bfloat16)
+        return carry
+
+    lax.fori_loop(0, width // tile, back_body, 0)
+    move_d = exchange(2, send.at[2])
+
+    rows_y = landed(1, move_y)
+
+    def front_body(n, carry):
+        at = pl.multiple_of(n * tile, tile)
+        proj_ref[:, pl.ds(at, tile)] = times(rows_y, w_all[:, pl.ds(at, tile)]).astype(
+            jnp.bfloat16
+        )
+        return carry
+
+    lax.fori_loop(0, w_ref.shape[1] // tile, front_body, 0)
+
+    grid_d = times(to_cells, landed(2, move_d)).astype(jnp.bfloat16)
+    halo_start(1, grid_d)
+    fill(field_d, own_layers, grid_d)
+    kernel_sums()
+
+    partners = [{"seq": sibling}, {"dp": 1 - plane}]
+    bit = 2
+    while bit < count:
+        partners.append({"seq": me + bit - 2 * bit * (me // bit % 2)})
+        bit *= 2
+
+    def sum_copy(stage):
+        copy = remote(
+            sums.at[stage], arrived.at[stage], sum_s.at[stage], sum_r.at[stage], partners[stage]
+        )
+        copy.start()
+        sent.append(copy)
+        return copy
+
+    summing = sum_copy(0)
+    halo_finish(1, field_d)
+    convolve(field_d, True)
+    move_b = outgoing(3, times(to_slots, cells[...]))
+    for stage in range(len(partners)):
+        summing.wait_recv()
+        if stage + 1 < len(partners):
+            sums[stage + 1] = sums[stage] + arrived[stage]
+            summing = sum_copy(stage + 1)
+        else:
+            dker_ref[...] = sums[stage] + arrived[stage]
+    dtok_ref[...] = landed(3, move_b)
+    for copy in sent:
+        copy.wait_send()
+
+
+def fused_shards(tokens, place, kernel, proj_weight, d_projected):
+    count = lax.axis_size("seq")
+    tokens_dev, width = tokens.shape[1:]
+    columns = proj_weight.shape[1]
+    layer = INLINE * CROSS
+    group = tokens_dev // count
+    depth = tokens_dev // layer
+    stages = count.bit_length()
+    line = count // 4
+    taps = kernel.shape[0]
+    vmem = pl.BlockSpec(memory_space=pltpu.VMEM)
+    dma = pltpu.SemaphoreType.DMA
+    bf16, f32 = (jnp.bfloat16, jnp.float32)
+    projected, d_tokens, d_kernel = pl.pallas_call(
+        functools.partial(fused, count),
+        out_shape=(
+            jax.ShapeDtypeStruct((tokens_dev, columns), bf16),
+            jax.ShapeDtypeStruct((tokens_dev, width), bf16),
+            jax.ShapeDtypeStruct((taps, width), f32),
+        ),
+        in_specs=[vmem] * 6,
+        out_specs=(vmem, vmem, vmem),
+        scratch_shapes=[
+            pltpu.VMEM((width, columns), bf16),
+            pltpu.VMEM((4, count, group, width), bf16),
+            pltpu.VMEM((4, count, group, width), bf16),
+            pltpu.VMEM((2, 2, layer, width), bf16),
+            pltpu.VMEM((2, 2, layer, width), bf16),
+            pltpu.VMEM((3, depth + 2, INLINE + 2, CROSS, width), f32),
+            pltpu.VMEM((3, depth + 2, INLINE + 2, CROSS, width), f32),
+            pltpu.VMEM((tokens_dev, width), bf16),
+            pltpu.VMEM((stages, taps, width), f32),
+            pltpu.VMEM((stages, taps, width), f32),
+            dma((4, count)),
+            dma((4, count)),
+            dma((2, line + 1, 2)),
+            dma((2, line + 1, 2)),
+            dma((2, line + 1)),
+            dma((2, line + 1)),
+            dma((3, line + 1, 3)),
+            dma((3, line + 1, 3)),
+            dma((2, 2)),
+            dma((2, 2)),
+            dma((stages,)),
+            dma((stages,)),
+        ],
+        compiler_params=pltpu.CompilerParams(
+            collective_id=0, has_side_effects=True, vmem_limit_bytes=56 * 1024 * 1024
+        ),
+        cost_estimate=pl.CostEstimate(
+            flops=4 * tokens_dev * width * columns,
+            bytes_accessed=4 * tokens_dev * columns,
+            transcendentals=0,
+        ),
+    )(
+        tokens[0].reshape(count, group, width),
+        place,
+        place.reshape(tokens_dev, 1),
+        kernel,
+        proj_weight,
+        d_projected[0],
+    )
+    return (projected[None], d_tokens[None], d_kernel)
+
+
 def solution(mesh):
     placed = (P("dp", "seq", None), P("seq", None), P(), P("seq", None), P("dp", "seq", None))
+    count = mesh.shape["seq"]
+    use_kernel = mesh.shape["dp"] == 2 and count == 16
     return jax.shard_map(
-        shards,
+        fused_shards if use_kernel else shards,
         mesh=mesh,
         in_specs=placed,
         out_specs=(P("dp", "seq", None), P("dp", "seq", None), P()),

time: 309 us -> 116 us (0.38)
  waiting for transfers between devices: 214 us -> 0 us
  Pallas kernels: 0 us -> 109 us
  starting transfers between devices: 30.2 us -> 0 us
  other arithmetic: 18.7 us -> 0 us
  matrix products: 14 us -> 0 us
  between operations: 14.6 us -> 0.66 us
  local copies, waits for them, and re-layouts: 14.6 us -> 5.35 us
    psum x1 -> x0, waiting for transfers between devices: 119 us -> none  [shards(): d_kernel = lax.psum(partial_value, ('dp', 'seq'))]
    pallas_call x0 -> x1, Pallas kernels: none -> 109 us  [fused_shards(): pl.pallas_call(functools.partial(fused, count), out_shape=(jax.ShapeDtype...]
    all_gather x1 -> x0, waiting for transfers between devices: 77 us -> none  [shards(): lax.all_gather(proj_weight, 'seq', axis=0, tiled=True)]
    all_to_all x4 -> x0, starting transfers between devices: 22.1 us -> none  [the longest x2 11.1 us: to_scan(): lax.all_to_all(scan_pieces(cells, order, count), 'seq', split_axis=0, con...]
    all_to_all x4 -> x0, waiting for transfers between devices: 17.5 us -> none  [the longest x2 9.31 us: to_scan(): lax.all_to_all(scan_pieces(cells, order, count), 'seq', split_axis=0, con...]
    dot_general x2 -> x0, matrix products: 14 us -> none  [the longest x1 7.77 us: shards(): lax.dot_general(d_rows, lax.all_gather(proj_weight, 'seq', axis=0, tiled=...]
    ppermute x4 -> x0, starting transfers between devices: 8.06 us -> none  [the longest x2 5.49 us: with_halo(): before = lax.ppermute(last, axis, up)]
    convert_element_type x2 -> x0, other arithmetic: 5.88 us -> none  [the longest x1 3.43 us: backward_conv(): return (back.astype(jnp.bfloat16), jnp.stack(partial_value))]
  transfers between devices with their start and end apart: 10 -> 0, of which waited for: 5 -> 0; matrix products, arithmetic and copies ran while one was open for 11% -> 0% of each run, Pallas kernels for 0% -> 0%
where the time goes in v1:
time: 116 us; the launch traced here: 115 us
  Pallas kernels  109 us (94%)
  local copies, waits for them, and re-layouts  5.35 us (5%)
    pallas_call x1, Pallas kernels, fused_shards(): pl.pallas_call(functools.partial(fused, count), out_shape=(jax.ShapeDtype...  109 us
    unnamed x9, local copies, waits for them, and re-layouts  4.61 us

profile of v1, /device:TPU:0, one launch (start us, length us, event | category | flops | bytes accessed | tf_op | source)
XLA Modules:
  0.0 114.8 jit_solution(1597887603378059127)
XLA Ops:
  0.6 0.0 copy-start.2
  0.6 0.6 copy-done.2
  1.3 0.7 copy.8.col_ref
  2.0 108.8 %shard_map.76 = (bf16[128,3840]{1,0:T(8,128)(2,1)}, bf16[128,1280]{1,0:T(8,128)(2,1)}, f32[27,1280]{1,0:T(8,128)}) custom-call(bf16[16,8,1280]{2,1,0:T(8,128)(2,1)} %bitcast.9, s32[1,128]{1,0:T(1,128)} %row_ref.1, s32[128,1]{1,0:T(8,128)} %copy.8.col_ref, f32[27,1280]{1,0:T(8,128)} %ker_ref.1, bf16[80,3840]{1,0:T(8,128)(2,1)} %w_ref.1, bf16[128,3840]{1,0:T(8,128)(2,1)} %bitcast.8), custom_call_target="tpu_custom_call" | custom-call | flops 2516582400 | bytes 1966080 | tf_op jit(solution)/shard_map/pallas_call | solution.py:535
  110.8 0.0 copy-start
  110.8 2.3 %copy.12 = bf16[1,128,3840]{2,1,0:T(8,128)(2,1)} copy(bf16[1,128,3840]{2,1,0:T(8,128)(2,1)} %bitcast.5) | data formatting | bytes 1966080
  113.1 0.0 copy-done
  113.1 0.0 copy-start.1
  113.1 0.7 copy.13
  113.8 0.3 copy-done.1
  114.1 0.7 copy.14
Async XLA Ops:
  0.6 0.7 copy-start.2
  110.8 2.3 %copy-start = (bf16[128,1280]{1,0:T(8,128)(2,1)S(1)}, bf16[128,1280]{1,0:T(8,128)(2,1)}, u32[]{:S(2)}) copy-start(bf16[128,1280]{1,0:T(8,128)(2,1)} %get-tuple-element.7) | copy-start | bytes 983044
  113.1 1.0 copy-start.1

commit v2 on v1

--- a/solution.py
+++ b/solution.py
@@ -129,7 +129,6 @@
     count,
     tok_ref,
     row_ref,
-    col_ref,
     ker_ref,
     w_ref,
     dp_ref,
@@ -144,6 +143,8 @@
     field_x,
     field_d,
     cells,
+    turned,
+    back_rows,
     sums,
     arrived,
     move_s,
@@ -270,7 +271,7 @@
     moving = {}
     for way in range(2):
         moving[way, 1] = ring_copies(way, 1)
-    for piece in range(2):
+    for piece in (1, 0):
         for way in range(2):
             moving[way, 1][piece].start()
     for way in range(2):
@@ -280,7 +281,7 @@
     )
     own_copy.start()
     sent.append(own_copy)
-    to_sibling = [own_copy]
+    to_sibling = {(0, 0): [own_copy]}
     across = {}
 
     def sibling_copy(way, hop, piece, shard, start):
@@ -293,7 +294,7 @@
         )
         copy.start()
         sent.append(copy)
-        to_sibling.append(copy)
+        to_sibling.setdefault((way, hop), []).append(copy)
 
     def ring_step(hop):
         ways = [way for way in range(2) if hop <= hops[way]]
@@ -301,7 +302,7 @@
             if hop < hops[way]:
                 moving[way, hop + 1] = ring_copies(way, hop + 1)
                 sent.extend(moving[way, hop + 1])
-        for piece, start in enumerate((0, own_third)):
+        for piece, start in ((1, own_third), (0, 0)):
             for way in ways:
                 shard = at_ring(ring - signs[way] * hop)
                 moving[way, hop][piece].wait_recv()
@@ -334,8 +335,10 @@
     def ones_where(mask):
         return jnp.where(mask, 1.0, 0.0).astype(jnp.bfloat16)
 
-    to_cells = ones_where(jnp.broadcast_to(row_ref[...], square) == first)
-    to_slots = ones_where(jnp.broadcast_to(col_ref[...], square) == second)
+    chosen = jnp.where(jnp.broadcast_to(row_ref[...], square) == first, 1.0, 0.0)
+    to_cells = chosen.astype(jnp.bfloat16)
+    to_slots = chosen.T.astype(jnp.bfloat16)
+    same = ones_where(first == second)
     spot = first % CROSS
     shifts = (
         ones_where((second == first - 1) & (spot > 0)),
@@ -411,7 +414,7 @@
     def lanes_of(j):
         return pl.ds(pl.multiple_of(j * LANES, LANES), LANES)
 
-    def convolve(field, flip):
+    def convolve(field, flip, start, stop):
         def body(j, carry):
             lanes = lanes_of(j)
             total = window(field, 1, 1, 1, lanes)
@@ -423,7 +426,7 @@
             cells[:, lanes] = total.reshape(tokens_dev, LANES).astype(jnp.bfloat16)
             return carry
 
-        lax.fori_loop(0, width // LANES, body, 0)
+        lax.fori_loop(start, stop, body, 0)
 
     def kernel_sums():
         def body(j, carry):
@@ -439,50 +442,60 @@
 
         lax.fori_loop(0, width // LANES, body, 0)
 
+    tile = 2 * LANES
+    chunks = width // LANES
     own_layers = tuple(range(1, depth + 1))
+
+    def turn_body(n, carry):
+        at = pl.multiple_of(n * LANES, LANES)
+        turned[pl.ds(at, LANES), :] = (
+            dp_ref[:, pl.ds(at, LANES)].astype(jnp.float32).T.astype(jnp.bfloat16)
+        )
+        return carry
+
+    def back_chip(position):
+        at = pl.ds(pl.multiple_of(at_ring(position) // 2 * (2 * rows), 16), 2 * rows)
+        back_rows[at, :] = times(w_all[at, :], turned[...]).astype(jnp.bfloat16)
+
+    def back_step(hop):
+        for way in range(2):
+            for copy in to_sibling.get((way, hop), ()):
+                copy.wait_recv()
+        if hop <= min(hops):
+            back_chip(ring - hop)
+        if hop > 0:
+            back_chip(ring + hop)
+
+    lax.fori_loop(0, w_ref.shape[1] // LANES, turn_body, 0)
     clear(field_x)
     clear(field_d)
-
+    ring_step(1)
     grid_x = times(to_cells, landed(0, move_x)).astype(jnp.bfloat16)
     halo_start(0, grid_x)
     fill(field_x, own_layers, grid_x)
-    ring_step(1)
+    across_step(1)
+    back_step(0)
+    ring_step(2)
     halo_finish(0, field_x)
-    convolve(field_x, False)
-    move_y = outgoing(1, times(to_slots, cells[...]))
-    for hop in range(2, line + 1):
+    back_step(1)
+    across_step(2)
+    for hop in range(3, line + 1):
         ring_step(hop)
-        across_step(hop - 1)
-    across_step(line)
-    for copy in to_sibling:
-        copy.wait_recv()
-
-    tile = 2 * LANES
-
-    def back_body(n, carry):
-        at = pl.multiple_of(n * tile, tile)
-        part = lax.dot_general(
-            dp_ref[...],
-            w_all[pl.ds(at, tile), :],
+        back_step(hop - 1)
+        across_step(hop)
+    back_step(line)
+
+    move_d = outgoing(
+        2,
+        lax.dot_general(
+            same,
+            back_rows[...],
             (((1,), (1,)), ((), ())),
             preferred_element_type=jnp.float32,
-        )
-        send[2, :, :, pl.ds(at, tile)] = part.reshape(count, group, tile).astype(jnp.bfloat16)
-        return carry
-
-    lax.fori_loop(0, width // tile, back_body, 0)
-    move_d = exchange(2, send.at[2])
-
-    rows_y = landed(1, move_y)
-
-    def front_body(n, carry):
-        at = pl.multiple_of(n * tile, tile)
-        proj_ref[:, pl.ds(at, tile)] = times(rows_y, w_all[:, pl.ds(at, tile)]).astype(
-            jnp.bfloat16
-        )
-        return carry
-
-    lax.fori_loop(0, w_ref.shape[1] // tile, front_body, 0)
+        ),
+    )
+    convolve(field_x, False, 0, chunks)
+    move_y = outgoing(1, times(to_slots, cells[...]))
 
     grid_d = times(to_cells, landed(2, move_d)).astype(jnp.bfloat16)
     halo_start(1, grid_d)
@@ -494,6 +507,7 @@
     while bit < count:
         partners.append({"seq": me + bit - 2 * bit * (me // bit % 2)})
         bit *= 2
+    stages = len(partners)
 
     def sum_copy(stage):
         copy = remote(
@@ -503,17 +517,37 @@
         sent.append(copy)
         return copy
 
+    def sum_step(stage, copy):
+        copy.wait_recv()
+        if stage + 1 == stages:
+            dker_ref[...] = sums[stage] + arrived[stage]
+            return copy
+        sums[stage + 1] = sums[stage] + arrived[stage]
+        return sum_copy(stage + 1)
+
     summing = sum_copy(0)
     halo_finish(1, field_d)
-    convolve(field_d, True)
+    convolve(field_d, True, 0, chunks // 2)
+    summing = sum_step(0, summing)
+    convolve(field_d, True, chunks // 2, chunks)
     move_b = outgoing(3, times(to_slots, cells[...]))
-    for stage in range(len(partners)):
-        summing.wait_recv()
-        if stage + 1 < len(partners):
-            sums[stage + 1] = sums[stage] + arrived[stage]
-            summing = sum_copy(stage + 1)
-        else:
-            dker_ref[...] = sums[stage] + arrived[stage]
+    summing = sum_step(1, summing)
+
+    rows_y = landed(1, move_y)
+    tiles = w_ref.shape[1] // tile
+
+    def front_body(n, carry):
+        at = pl.multiple_of(n * tile, tile)
+        proj_ref[:, pl.ds(at, tile)] = times(rows_y, w_all[:, pl.ds(at, tile)]).astype(
+            jnp.bfloat16
+        )
+        return carry
+
+    for stage in range(2, stages):
+        part = (stage - 2, stage - 1)
+        low, high = [tiles * p // (stages - 2) for p in part]
+        lax.fori_loop(low, high, front_body, 0)
+        summing = sum_step(stage, summing)
     dtok_ref[...] = landed(3, move_b)
     for copy in sent:
         copy.wait_send()
@@ -539,7 +573,7 @@
             jax.ShapeDtypeStruct((tokens_dev, width), bf16),
             jax.ShapeDtypeStruct((taps, width), f32),
         ),
-        in_specs=[vmem] * 6,
+        in_specs=[vmem] * 5,
         out_specs=(vmem, vmem, vmem),
         scratch_shapes=[
             pltpu.VMEM((width, columns), bf16),
@@ -550,6 +584,8 @@
             pltpu.VMEM((3, depth + 2, INLINE + 2, CROSS, width), f32),
             pltpu.VMEM((3, depth + 2, INLINE + 2, CROSS, width), f32),
             pltpu.VMEM((tokens_dev, width), bf16),
+            pltpu.VMEM((columns, tokens_dev), bf16),
+            pltpu.VMEM((width, tokens_dev), bf16),
             pltpu.VMEM((stages, taps, width), f32),
             pltpu.VMEM((stages, taps, width), f32),
             dma((4, count)),
@@ -576,7 +612,6 @@
     )(
         tokens[0].reshape(count, group, width),
         place,
-        place.reshape(tokens_dev, 1),
         kernel,
         proj_weight,
         d_projected[0],

time: 116 us -> 106 us (0.914)
  Pallas kernels: 109 us -> 101 us
  local copies, waits for them, and re-layouts: 5.35 us -> 3.96 us
    pallas_call x1, Pallas kernels: 109 us -> 101 us  [fused_shards(): pl.pallas_call(functools.partial(fused, count), out_shape=(jax.ShapeDtype...]
    unnamed x9 -> x7, local copies, waits for them, and re-layouts: 4.61 us -> 3.96 us
where the time goes in v2:
time: 106 us
  Pallas kernels  101 us (95%)
  local copies, waits for them, and re-layouts  3.96 us (4%)
    pallas_call x1, Pallas kernels, fused_shards(): pl.pallas_call(functools.partial(fused, count), out_shape=(jax.ShapeDtype...  101 us
    unnamed x7, local copies, waits for them, and re-layouts  3.96 us

profile of v2, /device:TPU:0, one launch (start us, length us, event | category | flops | bytes accessed | tf_op | source)
XLA Modules:
  0.0 105.7 jit_solution(9698387461561948931)
XLA Ops:
  0.6 101.1 %shard_map.76 = (bf16[128,3840]{1,0:T(8,128)(2,1)}, bf16[128,1280]{1,0:T(8,128)(2,1)}, f32[27,1280]{1,0:T(8,128)}) custom-call(bf16[16,8,1280]{2,1,0:T(8,128)(2,1)} %bitcast.7, s32[1,128]{1,0:T(1,128)} %row_ref.1, f32[27,1280]{1,0:T(8,128)} %ker_ref.1, bf16[80,3840]{1,0:T(8,128)(2,1)} %w_ref.1, bf16[128,3840]{1,0:T(8,128)(2,1)} %bitcast.6), custom_call_target="tpu_custom_call" | custom-call | flops 2516582400 | bytes 1966080 | tf_op jit(solution)/shard_map/pallas_call | solution.py:569
  101.8 0.0 copy-start
  101.8 2.3 %copy.11 = bf16[1,128,3840]{2,1,0:T(8,128)(2,1)} copy(bf16[1,128,3840]{2,1,0:T(8,128)(2,1)} %bitcast.4) | data formatting | bytes 1966080
  104.0 0.0 copy-done
  104.0 0.0 copy-start.1
  104.0 0.7 copy.12
  104.8 0.3 copy-done.1
  105.1 0.7 copy.13
Async XLA Ops:
  101.8 2.3 %copy-start = (bf16[128,1280]{1,0:T(8,128)(2,1)S(1)}, bf16[128,1280]{1,0:T(8,128)(2,1)}, u32[]{:S(2)}) copy-start(bf16[128,1280]{1,0:T(8,128)(2,1)} %get-tuple-element.7) | copy-start | bytes 983044
  104.0 1.0 copy-start.1

commit v3 on v2

--- a/solution.py
+++ b/solution.py
@@ -147,6 +147,7 @@
     back_rows,
     sums,
     arrived,
+    total,
     move_s,
     move_r,
     ring_s,
@@ -247,8 +248,6 @@
         send[which] = slots.reshape(count, group, width).astype(jnp.bfloat16)
         return exchange(which, send.at[which])
 
-    move_x = exchange(0, tok_ref)
-
     hops = (line, chips - 1 - line)
     signs = (sign, -sign)
 
@@ -417,13 +416,13 @@
     def convolve(field, flip, start, stop):
         def body(j, carry):
             lanes = lanes_of(j)
-            total = window(field, 1, 1, 1, lanes)
+            result = window(field, 1, 1, 1, lanes)
             for offset in range(27):
                 z, i, c = (offset // 9, offset // 3 % 3, offset % 3)
                 if flip:
                     z, i, c = (2 - z, 2 - i, 2 - c)
-                total = total + ker_ref[pl.ds(offset, 1), lanes] * window(field, z, i, c, lanes)
-            cells[:, lanes] = total.reshape(tokens_dev, LANES).astype(jnp.bfloat16)
+                result = result + ker_ref[pl.ds(offset, 1), lanes] * window(field, z, i, c, lanes)
+            cells[:, lanes] = result.reshape(tokens_dev, LANES).astype(jnp.bfloat16)
             return carry
 
         lax.fori_loop(start, stop, body, 0)
@@ -470,19 +469,20 @@
     clear(field_x)
     clear(field_d)
     ring_step(1)
+    move_x = exchange(0, tok_ref)
+    back_step(0)
+    ring_step(2)
+    across_step(1)
     grid_x = times(to_cells, landed(0, move_x)).astype(jnp.bfloat16)
     halo_start(0, grid_x)
     fill(field_x, own_layers, grid_x)
-    across_step(1)
-    back_step(0)
-    ring_step(2)
-    halo_finish(0, field_x)
-    back_step(1)
-    across_step(2)
     for hop in range(3, line + 1):
         ring_step(hop)
-        back_step(hop - 1)
-        across_step(hop)
+        across_step(hop - 1)
+        back_step(hop - 2)
+    halo_finish(0, field_x)
+    back_step(line - 1)
+    across_step(line)
     back_step(line)
 
     move_d = outgoing(
@@ -500,38 +500,68 @@
     grid_d = times(to_cells, landed(2, move_d)).astype(jnp.bfloat16)
     halo_start(1, grid_d)
     fill(field_d, own_layers, grid_d)
+    sums[0, pl.ds(3 * CROSS, CROSS)] = jnp.zeros((CROSS, width), jnp.float32)
     kernel_sums()
 
-    partners = [{"seq": sibling}, {"dp": 1 - plane}]
+    half, quarter = (2 * CROSS, CROSS)
+    core_rows = pl.multiple_of(core * half, CROSS)
+    far_core_rows = pl.multiple_of((1 - core) * half, CROSS)
+    plane_rows = pl.multiple_of(plane * quarter, CROSS)
+    far_plane_rows = pl.multiple_of((1 - plane) * quarter, CROSS)
+    home = pl.multiple_of(core * half + plane * quarter, CROSS)
+    partners = []
     bit = 2
     while bit < count:
         partners.append({"seq": me + bit - 2 * bit * (me // bit % 2)})
         bit *= 2
-    stages = len(partners)
+    stages = len(partners) + 4
 
     def sum_copy(stage):
-        copy = remote(
-            sums.at[stage], arrived.at[stage], sum_s.at[stage], sum_r.at[stage], partners[stage]
-        )
+        if stage == 0:
+            src, dst = (sums.at[0, pl.ds(far_core_rows, half)], arrived.at[0, pl.ds(0, half)])
+            target = {"seq": sibling}
+        elif stage == 1:
+            src, dst = (sums.at[1, pl.ds(far_plane_rows, quarter)], arrived.at[1, pl.ds(0, quarter)])
+            target = {"dp": 1 - plane}
+        elif stage < stages - 2:
+            src, dst = (sums.at[stage, pl.ds(0, quarter)], arrived.at[stage, pl.ds(0, quarter)])
+            target = partners[stage - 2]
+        elif stage == stages - 2:
+            src = dst = total.at[pl.ds(home, quarter)]
+            target = {"dp": 1 - plane}
+        else:
+            src = dst = total.at[pl.ds(core_rows, half)]
+            target = {"seq": sibling}
+        copy = remote(src, dst, sum_s.at[stage], sum_r.at[stage], target)
         copy.start()
         sent.append(copy)
         return copy
 
     def sum_step(stage, copy):
         copy.wait_recv()
-        if stage + 1 == stages:
-            dker_ref[...] = sums[stage] + arrived[stage]
-            return copy
-        sums[stage + 1] = sums[stage] + arrived[stage]
-        return sum_copy(stage + 1)
+        if stage == 0:
+            own = sums[0, pl.ds(core_rows, half)]
+            sums[1, pl.ds(0, half)] = own + arrived[0, pl.ds(0, half)]
+        elif stage < stages - 2:
+            own = sums[stage, pl.ds(plane_rows if stage == 1 else 0, quarter)]
+            added = own + arrived[stage, pl.ds(0, quarter)]
+            if stage + 1 == stages - 2:
+                total[pl.ds(home, quarter)] = added
+            else:
+                sums[stage + 1, pl.ds(0, quarter)] = added
+        if stage + 1 < stages:
+            return sum_copy(stage + 1)
+        dker_ref[...] = total[: dker_ref.shape[0]]
+        return copy
 
     summing = sum_copy(0)
     halo_finish(1, field_d)
     convolve(field_d, True, 0, chunks // 2)
     summing = sum_step(0, summing)
     convolve(field_d, True, chunks // 2, chunks)
+    summing = sum_step(1, summing)
     move_b = outgoing(3, times(to_slots, cells[...]))
-    summing = sum_step(1, summing)
+    summing = sum_step(2, summing)
 
     rows_y = landed(1, move_y)
     tiles = w_ref.shape[1] // tile
@@ -543,9 +573,8 @@
         )
         return carry
 
-    for stage in range(2, stages):
-        part = (stage - 2, stage - 1)
-        low, high = [tiles * p // (stages - 2) for p in part]
+    for stage in range(3, stages):
+        low, high = [tiles * part // (stages - 3) for part in (stage - 3, stage - 2)]
         lax.fori_loop(low, high, front_body, 0)
         summing = sum_step(stage, summing)
     dtok_ref[...] = landed(3, move_b)
@@ -560,7 +589,7 @@
     layer = INLINE * CROSS
     group = tokens_dev // count
     depth = tokens_dev // layer
-    stages = count.bit_length()
+    stages = count.bit_length() + 2
     line = count // 4
     taps = kernel.shape[0]
     vmem = pl.BlockSpec(memory_space=pltpu.VMEM)
@@ -586,8 +615,9 @@
             pltpu.VMEM((tokens_dev, width), bf16),
             pltpu.VMEM((columns, tokens_dev), bf16),
             pltpu.VMEM((width, tokens_dev), bf16),
-            pltpu.VMEM((stages, taps, width), f32),
-            pltpu.VMEM((stages, taps, width), f32),
+            pltpu.VMEM((stages, 4 * CROSS, width), f32),
+            pltpu.VMEM((stages, 4 * CROSS, width), f32),
+            pltpu.VMEM((4 * CROSS, width), f32),
             dma((4, count)),
             dma((4, count)),
             dma((2, line + 1, 2)),

time: 106 us -> 99.4 us (0.938)
  Pallas kernels: 101 us -> 94.6 us
    pallas_call x1, Pallas kernels: 101 us -> 94.6 us  [fused_shards(): pl.pallas_call(functools.partial(fused, count), out_shape=(jax.ShapeDtype...]
where the time goes in v3:
time: 99.4 us; the launch traced here: 99.2 us
  Pallas kernels  94.6 us (95%)
  local copies, waits for them, and re-layouts  3.96 us (4%)
    pallas_call x1, Pallas kernels, fused_shards(): pl.pallas_call(functools.partial(fused, count), out_shape=(jax.ShapeDtype...  94.6 us
    unnamed x7, local copies, waits for them, and re-layouts  3.96 us

profile of v3, /device:TPU:0, one launch (start us, length us, event | category | flops | bytes accessed | tf_op | source)
XLA Modules:
  0.0 99.2 jit_solution(190337986749864857)
XLA Ops:
  0.6 94.6 %shard_map.76 = (bf16[128,3840]{1,0:T(8,128)(2,1)}, bf16[128,1280]{1,0:T(8,128)(2,1)}, f32[27,1280]{1,0:T(8,128)}) custom-call(bf16[16,8,1280]{2,1,0:T(8,128)(2,1)} %bitcast.7, s32[1,128]{1,0:T(1,128)} %row_ref.1, f32[27,1280]{1,0:T(8,128)} %ker_ref.1, bf16[80,3840]{1,0:T(8,128)(2,1)} %w_ref.1, bf16[128,3840]{1,0:T(8,128)(2,1)} %bitcast.6), custom_call_target="tpu_custom_call" | custom-call | flops 2516582400 | bytes 1966080 | tf_op jit(solution)/shard_map/pallas_call | solution.py:598
  95.2 0.0 copy-start
  95.3 2.3 %copy.11 = bf16[1,128,3840]{2,1,0:T(8,128)(2,1)} copy(bf16[1,128,3840]{2,1,0:T(8,128)(2,1)} %bitcast.4) | data formatting | bytes 1966080
  97.5 0.0 copy-done
  97.5 0.0 copy-start.1
  97.5 0.7 copy.12
  98.2 0.3 copy-done.1
  98.5 0.7 copy.13
Async XLA Ops:
  95.2 2.3 %copy-start = (bf16[128,1280]{1,0:T(8,128)(2,1)S(1)}, bf16[128,1280]{1,0:T(8,128)(2,1)}, u32[]{:S(2)}) copy-start(bf16[128,1280]{1,0:T(8,128)(2,1)} %get-tuple-element.7) | copy-start | bytes 983044
  97.5 1.0 %copy-start.1 = (f32[27,1280]{1,0:T(8,128)S(1)}, f32[27,1280]{1,0:T(8,128)}, u32[]{:S(2)}) copy-start(f32[27,1280]{1,0:T(8,128)} %get-tuple-element.14) | copy-start | bytes 414724

commit v4 on v2

--- a/solution.py
+++ b/solution.py
@@ -147,6 +147,9 @@
     back_rows,
     sums,
     arrived,
+    paired,
+    layers,
+    total,
     move_s,
     move_r,
     ring_s,
@@ -214,7 +217,10 @@
             barrier, inc=1, device_id={"seq": (me + step) % count}, device_id_type=MESH
         )
     pl.semaphore_signal(barrier, inc=1, device_id={"dp": 1 - plane}, device_id_type=MESH)
-    pl.semaphore_wait(barrier, count)
+    pl.semaphore_signal(
+        barrier, inc=1, device_id={"dp": 1 - plane, "seq": sibling}, device_id_type=MESH
+    )
+    pl.semaphore_wait(barrier, count + 1)
 
     sent = []
 
@@ -246,8 +252,6 @@
     def outgoing(which, slots):
         send[which] = slots.reshape(count, group, width).astype(jnp.bfloat16)
         return exchange(which, send.at[which])
-
-    move_x = exchange(0, tok_ref)
 
     hops = (line, chips - 1 - line)
     signs = (sign, -sign)
@@ -417,13 +421,13 @@
     def convolve(field, flip, start, stop):
         def body(j, carry):
             lanes = lanes_of(j)
-            total = window(field, 1, 1, 1, lanes)
+            result = window(field, 1, 1, 1, lanes)
             for offset in range(27):
                 z, i, c = (offset // 9, offset // 3 % 3, offset % 3)
                 if flip:
                     z, i, c = (2 - z, 2 - i, 2 - c)
-                total = total + ker_ref[pl.ds(offset, 1), lanes] * window(field, z, i, c, lanes)
-            cells[:, lanes] = total.reshape(tokens_dev, LANES).astype(jnp.bfloat16)
+                result = result + ker_ref[pl.ds(offset, 1), lanes] * window(field, z, i, c, lanes)
+            cells[:, lanes] = result.reshape(tokens_dev, LANES).astype(jnp.bfloat16)
             return carry
 
         lax.fori_loop(start, stop, body, 0)
@@ -435,7 +439,7 @@
             for offset in range(27):
                 z, i, c = (offset // 9, offset // 3 % 3, offset % 3)
                 product = grad * window(field_x, z, i, c, lanes)
-                sums[0, pl.ds(offset, 1), lanes] = jnp.sum(
+                sums[pl.ds(offset, 1), lanes] = jnp.sum(
                     product.reshape(tokens_dev, LANES), axis=0, keepdims=True
                 )
             return carry
@@ -470,19 +474,20 @@
     clear(field_x)
     clear(field_d)
     ring_step(1)
+    move_x = exchange(0, tok_ref)
+    back_step(0)
+    ring_step(2)
+    across_step(1)
     grid_x = times(to_cells, landed(0, move_x)).astype(jnp.bfloat16)
     halo_start(0, grid_x)
     fill(field_x, own_layers, grid_x)
-    across_step(1)
-    back_step(0)
-    ring_step(2)
-    halo_finish(0, field_x)
-    back_step(1)
-    across_step(2)
     for hop in range(3, line + 1):
         ring_step(hop)
-        back_step(hop - 1)
-        across_step(hop)
+        across_step(hop - 1)
+        back_step(hop - 2)
+    halo_finish(0, field_x)
+    back_step(line - 1)
+    across_step(line)
     back_step(line)
 
     move_d = outgoing(
@@ -500,38 +505,89 @@
     grid_d = times(to_cells, landed(2, move_d)).astype(jnp.bfloat16)
     halo_start(1, grid_d)
     fill(field_d, own_layers, grid_d)
+    sums[pl.ds(3 * CROSS, CROSS)] = jnp.zeros((CROSS, width), jnp.float32)
     kernel_sums()
 
-    partners = [{"seq": sibling}, {"dp": 1 - plane}]
-    bit = 2
-    while bit < count:
-        partners.append({"seq": me + bit - 2 * bit * (me // bit % 2)})
-        bit *= 2
-    stages = len(partners)
-
-    def sum_copy(stage):
-        copy = remote(
-            sums.at[stage], arrived.at[stage], sum_s.at[stage], sum_r.at[stage], partners[stage]
-        )
-        copy.start()
-        sent.append(copy)
-        return copy
-
-    def sum_step(stage, copy):
-        copy.wait_recv()
-        if stage + 1 == stages:
-            dker_ref[...] = sums[stage] + arrived[stage]
-            return copy
-        sums[stage + 1] = sums[stage] + arrived[stage]
-        return sum_copy(stage + 1)
-
-    summing = sum_copy(0)
+    def start_all(copies):
+        for copy in copies:
+            copy.start()
+        sent.extend(copies)
+        return copies
+
+    def part_rows(core_at, plane_at):
+        return pl.ds(pl.multiple_of((core_at * 2 + plane_at) * CROSS, CROSS), CROSS)
+
+    home = part_rows(core, plane)
+    squad = (
+        (1 - core, plane, {"seq": sibling}),
+        (core, 1 - plane, {"dp": 1 - plane}),
+        (1 - core, 1 - plane, {"dp": 1 - plane, "seq": sibling}),
+    )
+
+    def scatter_sums():
+        return start_all(
+            [
+                remote(
+                    sums.at[part_rows(core_at, plane_at)],
+                    arrived.at[k],
+                    sum_s.at[0, k],
+                    sum_r.at[0, k],
+                    target,
+                )
+                for k, (core_at, plane_at, target) in enumerate(squad)
+            ]
+        )
+
+    def pair_sums(copies):
+        for copy in copies:
+            copy.wait_recv()
+        paired[...] = sums[home] + arrived[0] + arrived[1] + arrived[2]
+        target = {"seq": me + 2 - 4 * chip_y}
+        return start_all([remote(paired, arrived.at[3], sum_s.at[1, 0], sum_r.at[1, 0], target)])
+
+    def line_sums(copies):
+        for copy in copies:
+            copy.wait_recv()
+        layers[chip_z] = paired[...] + arrived[3]
+        return start_all(
+            [
+                remote(
+                    layers.at[chip_z],
+                    layers.at[chip_z],
+                    sum_s.at[2, k],
+                    sum_r.at[2, k],
+                    {"seq": (chip_z + k) % line * 4 + chip_y * 2 + core},
+                )
+                for k in range(1, line)
+            ]
+        )
+
+    def share_sums(copies):
+        for copy in copies:
+            copy.wait_recv()
+        whole_sum = layers[0]
+        for k in range(1, line):
+            whole_sum = whole_sum + layers[k]
+        total[home] = whole_sum
+        return start_all(
+            [
+                remote(total.at[home], total.at[home], sum_s.at[3, k], sum_r.at[3, k], target)
+                for k, (core_at, plane_at, target) in enumerate(squad)
+            ]
+        )
+
+    def finish_sums(copies):
+        for copy in copies:
+            copy.wait_recv()
+        dker_ref[...] = total[: dker_ref.shape[0]]
+
+    summing = scatter_sums()
     halo_finish(1, field_d)
     convolve(field_d, True, 0, chunks // 2)
-    summing = sum_step(0, summing)
+    summing = pair_sums(summing)
     convolve(field_d, True, chunks // 2, chunks)
+    summing = line_sums(summing)
     move_b = outgoing(3, times(to_slots, cells[...]))
-    summing = sum_step(1, summing)
 
     rows_y = landed(1, move_y)
     tiles = w_ref.shape[1] // tile
@@ -543,14 +599,29 @@
         )
         return carry
 
-    for stage in range(2, stages):
-        part = (stage - 2, stage - 1)
-        low, high = [tiles * p // (stages - 2) for p in part]
-        lax.fori_loop(low, high, front_body, 0)
-        summing = sum_step(stage, summing)
+    lax.fori_loop(0, tiles // 2, front_body, 0)
+    summing = share_sums(summing)
+    lax.fori_loop(tiles // 2, tiles, front_body, 0)
+    finish_sums(summing)
     dtok_ref[...] = landed(3, move_b)
     for copy in sent:
         copy.wait_send()
+
+
+def copy_results(proj_in, dtok_in, dker_in, proj_out, dtok_out, dker_out, sems):
+    half = pl.ds(0, proj_in.shape[0] // 2)
+    rest = pl.ds(proj_in.shape[0] // 2, proj_in.shape[0] // 2)
+    pairs = (
+        (proj_in.at[half], proj_out.at[half]),
+        (proj_in.at[rest], proj_out.at[rest]),
+        (dtok_in, dtok_out),
+        (dker_in, dker_out),
+    )
+    copies = [pltpu.make_async_copy(src, dst, sems.at[k]) for k, (src, dst) in enumerate(pairs)]
+    for copy in copies:
+        copy.start()
+    for copy in copies:
+        copy.wait()
 
 
 def fused_shards(tokens, place, kernel, proj_weight, d_projected):
@@ -560,7 +631,6 @@
     layer = INLINE * CROSS
     group = tokens_dev // count
     depth = tokens_dev // layer
-    stages = count.bit_length()
     line = count // 4
     taps = kernel.shape[0]
     vmem = pl.BlockSpec(memory_space=pltpu.VMEM)
@@ -586,8 +656,11 @@
             pltpu.VMEM((tokens_dev, width), bf16),
             pltpu.VMEM((columns, tokens_dev), bf16),
             pltpu.VMEM((width, tokens_dev), bf16),
-            pltpu.VMEM((stages, taps, width), f32),
-            pltpu.VMEM((stages, taps, width), f32),
+            pltpu.VMEM((4 * CROSS, width), f32),
+            pltpu.VMEM((4, CROSS, width), f32),
+            pltpu.VMEM((CROSS, width), f32),
+            pltpu.VMEM((line, CROSS, width), f32),
+            pltpu.VMEM((4 * CROSS, width), f32),
             dma((4, count)),
             dma((4, count)),
             dma((2, line + 1, 2)),
@@ -598,8 +671,8 @@
             dma((3, line + 1, 3)),
             dma((2, 2)),
             dma((2, 2)),
-            dma((stages,)),
-            dma((stages,)),
+            dma((4, 4)),
+            dma((4, 4)),
         ],
         compiler_params=pltpu.CompilerParams(
             collective_id=0, has_side_effects=True, vmem_limit_bytes=56 * 1024 * 1024
@@ -616,6 +689,15 @@
         proj_weight,
         d_projected[0],
     )
+    results = [projected, d_tokens, d_kernel]
+    anywhere = pl.BlockSpec(memory_space=pl.ANY)
+    projected, d_tokens, d_kernel = pl.pallas_call(
+        copy_results,
+        out_shape=tuple(jax.ShapeDtypeStruct(r.shape, r.dtype) for r in results),
+        in_specs=[anywhere] * 3,
+        out_specs=(anywhere,) * 3,
+        scratch_shapes=[dma((4,))],
+    )(*results)
     return (projected[None], d_tokens[None], d_kernel)
 
 

time: 106 us -> 136 us (1.28)
  Pallas kernels: 101 us -> 135 us
  local copies, waits for them, and re-layouts: 3.96 us -> 0 us
    pallas_call x0 -> x1, Pallas kernels: none -> 45.8 us  [fused_shards(): pl.pallas_call(copy_results, out_shape=tuple((jax.ShapeDtypeStruct(r.shap...]
    pallas_call x1, Pallas kernels: 101 us -> 89.6 us  [fused_shards(): pl.pallas_call(functools.partial(fused, count), out_shape=(jax.ShapeDtype...]
    unnamed x7 -> x0, local copies, waits for them, and re-layouts: 3.96 us -> none
where the time goes in v4:
time: 136 us
  Pallas kernels  135 us (99%)
    pallas_call x1, Pallas kernels, fused_shards(): pl.pallas_call(functools.partial(fused, count), out_shape=(jax.ShapeDtype...  89.6 us
    pallas_call x1, Pallas kernels, fused_shards(): pl.pallas_call(copy_results, out_shape=tuple((jax.ShapeDtypeStruct(r.shap...  45.8 us

profile of v4, /device:TPU:0, one launch (start us, length us, event | category | flops | bytes accessed | tf_op | source)
XLA Modules:
  0.0 136.0 jit_solution(14220925276320349513)
XLA Ops:
  0.6 89.6 %shard_map.76 = (bf16[128,3840]{1,0:T(8,128)(2,1)}, bf16[128,1280]{1,0:T(8,128)(2,1)}, f32[27,1280]{1,0:T(8,128)}) custom-call(bf16[16,8,1280]{2,1,0:T(8,128)(2,1)} %bitcast.6, s32[1,128]{1,0:T(1,128)} %row_ref.1, f32[27,1280]{1,0:T(8,128)} %ker_ref.1, bf16[80,3840]{1,0:T(8,128)(2,1)} %w_ref.1, bf16[128,3840]{1,0:T(8,128)(2,1)} %bitcast.4), custom_call_target="tpu_custom_call" | custom-call | flops 2516582400 | bytes 1966080 | tf_op jit(solution)/shard_map/pallas_call | solution.py:639
  90.2 45.8 %shard_map.77 = (bf16[128,3840]{1,0:T(8,128)(2,1)}, bf16[128,1280]{1,0:T(8,128)(2,1)}, f32[27,1280]{1,0:T(8,128)}) custom-call(bf16[128,3840]{1,0:T(8,128)(2,1)} %get-tuple-element.9.proj_in, bf16[128,1280]{1,0:T(8,128)(2,1)} %get-tuple-element.10.dtok_in, f32[27,1280]{1,0:T(8,128)} %get-tuple-element.11.dker_in), custom_call_target="tpu_custom_call" | custom-call | tf_op jit(solution)/shard_map/pallas_call | solution.py:694

commit v5 on v4

--- a/solution.py
+++ b/solution.py
@@ -189,8 +189,12 @@
         z = spot * (1 - side) + (chips - 1 - spot) * side
         return (z * 2 + side) * 2 + core
 
-    def block(shard, start):
-        return w_all.at[pl.ds(pl.multiple_of(shard * rows, 16), rows), pl.ds(start, third)]
+    upper = (rows // 32 + rows // 16 % 2) * 16
+    halves = ((0, upper), (upper, rows - upper))
+
+    def block(shard, start, half):
+        low, size = halves[half]
+        return w_all.at[pl.ds(pl.multiple_of(shard * rows + low, 16), size), pl.ds(start, third)]
 
     def whole(shard):
         return w_all.at[pl.ds(pl.multiple_of(shard * rows, 16), rows), :]
@@ -254,17 +258,18 @@
         return exchange(which, send.at[which])
 
     hops = (line, chips - 1 - line)
+    pieces = ((own_third, 0), (own_third, 1), (0, 0), (0, 1))
     signs = (sign, -sign)
 
     def ring_copies(way, hop):
         shard = at_ring(ring - signs[way] * (hop - 1))
         target = {"seq": at_ring(ring + signs[way])}
         pair = []
-        for piece, start in enumerate((0, own_third)):
+        for piece, (start, half) in enumerate(pieces):
             pair.append(
                 remote(
-                    block(shard, start),
-                    block(shard, start),
+                    block(shard, start, half),
+                    block(shard, start, half),
                     ring_s.at[way, hop, piece],
                     ring_r.at[way, hop, piece],
                     target,
@@ -275,7 +280,7 @@
     moving = {}
     for way in range(2):
         moving[way, 1] = ring_copies(way, 1)
-    for piece in (1, 0):
+    for piece in range(len(pieces)):
         for way in range(2):
             moving[way, 1][piece].start()
     for way in range(2):
@@ -288,10 +293,10 @@
     to_sibling = {(0, 0): [own_copy]}
     across = {}
 
-    def sibling_copy(way, hop, piece, shard, start):
+    def sibling_copy(way, hop, piece, shard, start, half):
         copy = remote(
-            block(shard, start),
-            block(shard, start),
+            block(shard, start, half),
+            block(shard, start, half),
             sib_s.at[1 + way, hop, piece],
             sib_r.at[1 + way, hop, piece],
             {"seq": sibling},
@@ -306,31 +311,32 @@
             if hop < hops[way]:
                 moving[way, hop + 1] = ring_copies(way, hop + 1)
                 sent.extend(moving[way, hop + 1])
-        for piece, start in ((1, own_third), (0, 0)):
+        for piece, (start, half) in enumerate(pieces):
             for way in ways:
                 shard = at_ring(ring - signs[way] * hop)
                 moving[way, hop][piece].wait_recv()
                 if hop < hops[way]:
                     moving[way, hop + 1][piece].start()
-                if piece == 1:
+                if piece < 2:
                     copy = remote(
-                        block(shard, start),
-                        block(shard, start),
-                        part_s.at[way, hop],
-                        part_r.at[way, hop],
+                        block(shard, start, half),
+                        block(shard, start, half),
+                        part_s.at[way, hop, half],
+                        part_r.at[way, hop, half],
                         {"dp": 1 - plane},
                     )
                     copy.start()
                     sent.append(copy)
-                    across[way, hop] = copy
-                sibling_copy(way, hop, piece, shard, start)
+                    across[way, hop, half] = copy
+                sibling_copy(way, hop, piece, shard, start, half)
 
     def across_step(hop):
-        for way in range(2):
-            if hop <= hops[way]:
-                shard = at_ring(ring - signs[way] * hop)
-                across[way, hop].wait_recv()
-                sibling_copy(way, hop, 2, shard, other_third)
+        for half in range(2):
+            for way in range(2):
+                if hop <= hops[way]:
+                    shard = at_ring(ring - signs[way] * hop)
+                    across[way, hop, half].wait_recv()
+                    sibling_copy(way, hop, 4 + half, shard, other_third, half)
 
     square = (tokens_dev, tokens_dev)
     first = lax.broadcasted_iota(jnp.int32, square, 0)
@@ -608,20 +614,10 @@
         copy.wait_send()
 
 
-def copy_results(proj_in, dtok_in, dker_in, proj_out, dtok_out, dker_out, sems):
-    half = pl.ds(0, proj_in.shape[0] // 2)
-    rest = pl.ds(proj_in.shape[0] // 2, proj_in.shape[0] // 2)
-    pairs = (
-        (proj_in.at[half], proj_out.at[half]),
-        (proj_in.at[rest], proj_out.at[rest]),
-        (dtok_in, dtok_out),
-        (dker_in, dker_out),
-    )
-    copies = [pltpu.make_async_copy(src, dst, sems.at[k]) for k, (src, dst) in enumerate(pairs)]
-    for copy in copies:
-        copy.start()
-    for copy in copies:
-        copy.wait()
+def copy_results(proj_in, dtok_in, dker_in, proj_out, dtok_out, dker_out):
+    proj_out[...] = proj_in[...]
+    dtok_out[...] = dtok_in[...]
+    dker_out[...] = dker_in[...]
 
 
 def fused_shards(tokens, place, kernel, proj_weight, d_projected):
@@ -663,12 +659,12 @@
             pltpu.VMEM((4 * CROSS, width), f32),
             dma((4, count)),
             dma((4, count)),
+            dma((2, line + 1, 4)),
+            dma((2, line + 1, 4)),
             dma((2, line + 1, 2)),
             dma((2, line + 1, 2)),
-            dma((2, line + 1)),
-            dma((2, line + 1)),
-            dma((3, line + 1, 3)),
-            dma((3, line + 1, 3)),
+            dma((3, line + 1, 6)),
+            dma((3, line + 1, 6)),
             dma((2, 2)),
             dma((2, 2)),
             dma((4, 4)),
@@ -690,13 +686,11 @@
         d_projected[0],
     )
     results = [projected, d_tokens, d_kernel]
-    anywhere = pl.BlockSpec(memory_space=pl.ANY)
     projected, d_tokens, d_kernel = pl.pallas_call(
         copy_results,
         out_shape=tuple(jax.ShapeDtypeStruct(r.shape, r.dtype) for r in results),
-        in_specs=[anywhere] * 3,
-        out_specs=(anywhere,) * 3,
-        scratch_shapes=[dma((4,))],
+        in_specs=[vmem] * 3,
+        out_specs=(vmem,) * 3,
     )(*results)
     return (projected[None], d_tokens[None], d_kernel)
 

time: 136 us -> 92.5 us (0.68)
  Pallas kernels: 135 us -> 91.7 us
    pallas_call x1, Pallas kernels: 45.8 us -> 2.43 us  [fused_shards(): pl.pallas_call(copy_results, out_shape=tuple((jax.ShapeDtypeStruct(r.shap...]
where the time goes in v5:
time: 92.5 us; the launch traced here: 92.3 us
  Pallas kernels  91.7 us (99%)
    pallas_call x1, Pallas kernels, fused_shards(): pl.pallas_call(functools.partial(fused, count), out_shape=(jax.ShapeDtype...  89.3 us
    pallas_call x1, Pallas kernels, fused_shards(): pl.pallas_call(copy_results, out_shape=tuple((jax.ShapeDtypeStruct(r.shap...  2.43 us

profile of v5, /device:TPU:0, one launch (start us, length us, event | category | flops | bytes accessed | tf_op | source)
XLA Modules:
  0.0 92.3 jit_solution(14286040152893054872)
XLA Ops:
  0.6 89.3 %shard_map.76 = (bf16[128,3840]{1,0:T(8,128)(2,1)}, bf16[128,1280]{1,0:T(8,128)(2,1)}, f32[27,1280]{1,0:T(8,128)}) custom-call(bf16[16,8,1280]{2,1,0:T(8,128)(2,1)} %bitcast.6, s32[1,128]{1,0:T(1,128)} %row_ref.1, f32[27,1280]{1,0:T(8,128)} %ker_ref.1, bf16[80,3840]{1,0:T(8,128)(2,1)} %w_ref.1, bf16[128,3840]{1,0:T(8,128)(2,1)} %bitcast.4), custom_call_target="tpu_custom_call" | custom-call | flops 2516582400 | bytes 1966080 | tf_op jit(solution)/shard_map/pallas_call | solution.py:635
  89.9 2.4 %shard_map.77 = (bf16[128,3840]{1,0:T(8,128)(2,1)}, bf16[128,1280]{1,0:T(8,128)(2,1)}, f32[27,1280]{1,0:T(8,128)}) custom-call(bf16[128,3840]{1,0:T(8,128)(2,1)} %get-tuple-element.9.proj_in, bf16[128,1280]{1,0:T(8,128)(2,1)} %get-tuple-element.10.dtok_in, f32[27,1280]{1,0:T(8,128)} %get-tuple-element.11.dker_in), custom_call_target="tpu_custom_call" | custom-call | tf_op jit(solution)/shard_map/pallas_call | solution.py:689

commit v6 on v5

--- a/solution.py
+++ b/solution.py
@@ -228,23 +228,25 @@
 
     sent = []
 
-    def exchange(which, source):
+    def exchange(which, source, lanes=None, row=None):
+        lanes = pl.ds(0, width) if lanes is None else lanes
+        row = which if row is None else row
         copies = []
         for step in range(1, count):
             target = (me + step) % count
             copies.append(
                 remote(
-                    source.at[target],
-                    land.at[which, me],
-                    move_s.at[which, step],
-                    move_r.at[which, step],
+                    source.at[target, :, lanes],
+                    land.at[which, me, :, lanes],
+                    move_s.at[row, step],
+                    move_r.at[row, step],
                     {"seq": target},
                 )
             )
         for copy in copies:
             copy.start()
         sent.extend(copies)
-        land[which, pl.ds(me, 1)] = source[pl.ds(me, 1)]
+        land[which, pl.ds(me, 1), :, lanes] = source[pl.ds(me, 1), :, lanes]
         return copies
 
     def landed(which, copies):
@@ -589,11 +591,20 @@
 
     summing = scatter_sums()
     halo_finish(1, field_d)
+    middle = chunks // 2 * LANES
+
+    def send_half(row, low, size):
+        lanes = pl.ds(low, size)
+        slots = times(to_slots, cells[:, lanes])
+        send[3, :, :, lanes] = slots.reshape(count, group, size).astype(jnp.bfloat16)
+        return exchange(3, send.at[3], lanes, row)
+
     convolve(field_d, True, 0, chunks // 2)
     summing = pair_sums(summing)
+    move_b = send_half(3, 0, middle)
     convolve(field_d, True, chunks // 2, chunks)
     summing = line_sums(summing)
-    move_b = outgoing(3, times(to_slots, cells[...]))
+    move_b = move_b + send_half(4, middle, width - middle)
 
     rows_y = landed(1, move_y)
     tiles = w_ref.shape[1] // tile
@@ -657,8 +668,8 @@
             pltpu.VMEM((CROSS, width), f32),
             pltpu.VMEM((line, CROSS, width), f32),
             pltpu.VMEM((4 * CROSS, width), f32),
-            dma((4, count)),
-            dma((4, count)),
+            dma((5, count)),
+            dma((5, count)),
             dma((2, line + 1, 4)),
             dma((2, line + 1, 4)),
             dma((2, line + 1, 2)),

time: 92.5 us -> 92.8 us (level)
  no operation moved by 1% of the time
where the time goes in v6:
time: 92.8 us; the launch traced here: 92.6 us
  Pallas kernels  92 us (99%)
    pallas_call x1, Pallas kernels, fused_shards(): pl.pallas_call(functools.partial(fused, count), out_shape=(jax.ShapeDtype...  89.6 us
    pallas_call x1, Pallas kernels, fused_shards(): pl.pallas_call(copy_results, out_shape=tuple((jax.ShapeDtypeStruct(r.shap...  2.43 us

profile of v6, /device:TPU:0, one launch (start us, length us, event | category | flops | bytes accessed | tf_op | source)
XLA Modules:
  0.0 92.6 jit_solution(2505841727122120572)
XLA Ops:
  0.6 89.6 %shard_map.76 = (bf16[128,3840]{1,0:T(8,128)(2,1)}, bf16[128,1280]{1,0:T(8,128)(2,1)}, f32[27,1280]{1,0:T(8,128)}) custom-call(bf16[16,8,1280]{2,1,0:T(8,128)(2,1)} %bitcast.6, s32[1,128]{1,0:T(1,128)} %row_ref.1, f32[27,1280]{1,0:T(8,128)} %ker_ref.1, bf16[80,3840]{1,0:T(8,128)(2,1)} %w_ref.1, bf16[128,3840]{1,0:T(8,128)(2,1)} %bitcast.4), custom_call_target="tpu_custom_call" | custom-call | flops 2516582400 | bytes 1966080 | tf_op jit(solution)/shard_map/pallas_call | solution.py:646
  90.2 2.4 %shard_map.77 = (bf16[128,3840]{1,0:T(8,128)(2,1)}, bf16[128,1280]{1,0:T(8,128)(2,1)}, f32[27,1280]{1,0:T(8,128)}) custom-call(bf16[128,3840]{1,0:T(8,128)(2,1)} %get-tuple-element.9.proj_in, bf16[128,1280]{1,0:T(8,128)(2,1)} %get-tuple-element.10.dtok_in, f32[27,1280]{1,0:T(8,128)} %get-tuple-element.11.dker_in), custom_call_target="tpu_custom_call" | custom-call | tf_op jit(solution)/shard_map/pallas_call | solution.py:700

commit v7 on v5

--- a/solution.py
+++ b/solution.py
@@ -491,7 +491,10 @@
         ring_step(hop)
         across_step(hop - 1)
         back_step(hop - 2)
-    halo_finish(0, field_x)
+        if hop == line - 1:
+            halo_finish(0, field_x)
+            convolve(field_x, False, 0, chunks)
+            move_y = outgoing(1, times(to_slots, cells[...]))
     back_step(line - 1)
     across_step(line)
     back_step(line)
@@ -505,8 +508,17 @@
             preferred_element_type=jnp.float32,
         ),
     )
-    convolve(field_x, False, 0, chunks)
-    move_y = outgoing(1, times(to_slots, cells[...]))
+    rows_y = landed(1, move_y)
+    tiles = w_ref.shape[1] // tile
+
+    def front_body(n, carry):
+        at = pl.multiple_of(n * tile, tile)
+        proj_ref[:, pl.ds(at, tile)] = times(rows_y, w_all[:, pl.ds(at, tile)]).astype(
+            jnp.bfloat16
+        )
+        return carry
+
+    lax.fori_loop(0, tiles // 2, front_body, 0)
 
     grid_d = times(to_cells, landed(2, move_d)).astype(jnp.bfloat16)
     halo_start(1, grid_d)
@@ -595,19 +607,9 @@
     summing = line_sums(summing)
     move_b = outgoing(3, times(to_slots, cells[...]))
 
-    rows_y = landed(1, move_y)
-    tiles = w_ref.shape[1] // tile
-
-    def front_body(n, carry):
-        at = pl.multiple_of(n * tile, tile)
-        proj_ref[:, pl.ds(at, tile)] = times(rows_y, w_all[:, pl.ds(at, tile)]).astype(
-            jnp.bfloat16
-        )
-        return carry
-
-    lax.fori_loop(0, tiles // 2, front_body, 0)
+    lax.fori_loop(tiles // 2, tiles * 3 // 4, front_body, 0)
     summing = share_sums(summing)
-    lax.fori_loop(tiles // 2, tiles, front_body, 0)
+    lax.fori_loop(tiles * 3 // 4, tiles, front_body, 0)
     finish_sums(summing)
     dtok_ref[...] = landed(3, move_b)
     for copy in sent:

time: 92.5 us -> 91.4 us (0.988)
  Pallas kernels: 91.7 us -> 90.6 us
    pallas_call x1, Pallas kernels: 89.3 us -> 88.2 us  [fused_shards(): pl.pallas_call(functools.partial(fused, count), out_shape=(jax.ShapeDtype...]
where the time goes in v7:
time: 91.4 us; the launch traced here: 91.3 us
  Pallas kernels  90.6 us (99%)
    pallas_call x1, Pallas kernels, fused_shards(): pl.pallas_call(functools.partial(fused, count), out_shape=(jax.ShapeDtype...  88.2 us
    pallas_call x1, Pallas kernels, fused_shards(): pl.pallas_call(copy_results, out_shape=tuple((jax.ShapeDtypeStruct(r.shap...  2.43 us

profile of v7, /device:TPU:0, one launch (start us, length us, event | category | flops | bytes accessed | tf_op | source)
XLA Modules:
  0.0 91.3 jit_solution(6799685496310169124)
XLA Ops:
  0.6 88.2 %shard_map.76 = (bf16[128,3840]{1,0:T(8,128)(2,1)}, bf16[128,1280]{1,0:T(8,128)(2,1)}, f32[27,1280]{1,0:T(8,128)}) custom-call(bf16[16,8,1280]{2,1,0:T(8,128)(2,1)} %bitcast.6, s32[1,128]{1,0:T(1,128)} %row_ref.1, f32[27,1280]{1,0:T(8,128)} %ker_ref.1, bf16[80,3840]{1,0:T(8,128)(2,1)} %w_ref.1, bf16[128,3840]{1,0:T(8,128)(2,1)} %bitcast.4), custom_call_target="tpu_custom_call" | custom-call | flops 2516582400 | bytes 1966080 | tf_op jit(solution)/shard_map/pallas_call | solution.py:637
  88.8 2.4 %shard_map.77 = (bf16[128,3840]{1,0:T(8,128)(2,1)}, bf16[128,1280]{1,0:T(8,128)(2,1)}, f32[27,1280]{1,0:T(8,128)}) custom-call(bf16[128,3840]{1,0:T(8,128)(2,1)} %get-tuple-element.9.proj_in, bf16[128,1280]{1,0:T(8,128)(2,1)} %get-tuple-element.10.dtok_in, f32[27,1280]{1,0:T(8,128)} %get-tuple-element.11.dker_in), custom_call_target="tpu_custom_call" | custom-call | tf_op jit(solution)/shard_map/pallas_call | solution.py:691
